TPU v7x, 256 devices: a whole 4x4x8 slice. The times are simulated.
256 devices in a mesh: vp: 64 (over y_hi, z, x), ch: 4 (over y_lo, core).
Axes of the slice: x: 4, y: 4 (y_hi: 2, y_lo: 2; y = y_hi * 2 + y_lo), z: 8, core: 2. Of those that a mesh axis runs over, the one named last changes fastest.
Arguments:
- chol_a: bfloat16 [640, 4, 6000], P('vp', None, 'ch'), may hold values from -0.078125 to 0.078125
- chol_b: bfloat16 [6000, 64, 640], P('ch', 'vp'), may hold values from -6 to 6
- amplitudes: bfloat16 [640, 8, 640], P('vp'), may hold values from -0.0390625 to 0.0390625
- vir_a: float32 [4], replicated, may hold values from 0.2 to 3
- vir_b: float32 [64], P('vp'), may hold values from 0.2 to 3
- occ_pair: float32 [8], P('ch'), may hold values from -4 to -1
Outputs:
- increment: float32 [4, 64, 8], P(None, 'vp', 'ch')
All inputs are finite; a program needn't handle non-finite values.
Results may differ from a plain program's by a relative error of at most 0.0029.
Values may be sent and summed in bfloat16 or wider, within the bound.
A program may use at most 64 MiB of HBM per device.

v0:
```python
import jax
import jax.numpy as jnp
from jax import lax
from jax.sharding import PartitionSpec as P


def body(chol_a, chol_b, amplitudes, vir_a, vir_b, occ_pair):
    nch_dev = chol_b.shape[0]
    nb_dev = chol_b.shape[1]
    vir_count = chol_b.shape[2]
    a_count = chol_a.shape[1]
    pair_count = amplitudes.shape[1]
    cholesky_right = chol_b.reshape(nch_dev, nb_dev * vir_count)
    panel_rows = lax.all_gather(chol_a, "vp", axis=0, tiled=True)
    rows_here = panel_rows.shape[0]
    v_rows = jnp.dot(
        panel_rows.reshape(rows_here * a_count, nch_dev),
        cholesky_right,
        preferred_element_type=jnp.float32,
    )
    v_all = v_rows.astype(jnp.bfloat16).reshape(rows_here, a_count * nb_dev, vir_count)
    v_rows = v_all
    ladder = jnp.einsum(
        "cxd,cid->xi",
        v_rows,
        lax.all_gather(amplitudes, "vp", axis=0, tiled=True),
        preferred_element_type=jnp.float32,
    )
    ladder = ladder.reshape(a_count, nb_dev, pair_count)
    ladder = lax.psum_scatter(ladder, "ch", scatter_dimension=2, tiled=True)
    energy_gap = vir_a[:, None, None] + vir_b[None, :, None] - occ_pair[None, None, :]
    return ladder / energy_gap


def solution(mesh):
    return jax.shard_map(
        body,
        mesh=mesh,
        in_specs=(
            P("vp", None, "ch"),
            P("ch", "vp", None),
            P("vp", None, None),
            P(),
            P("vp"),
            P("ch"),
        ),
        out_specs=P(None, "vp", "ch"),
        check_vma=False,
    )
```

profile of v0, /device:TPU:1, one launch (start us, length us, event | category | flops | bytes accessed | tf_op | source)
XLA Modules:
  0.0 319.8 jit_solution(13884789636193917193)
XLA Ops:
  6.5 0.0 copy-start
  6.5 0.0 all-gather.3.cloned.1.call-start
  6.5 0.7 all-gather.3.cloned.1.call-update
  7.3 0.0 all-gather.5.cloned.1.call-start
  7.3 0.7 all-gather.5.cloned.1.call-update
  8.7 1.3 dynamic-slice
  10.6 0.7 broadcast_add_fusion
  11.2 145.8 %all-gather.3.cloned.1.call-done = bf16[640,4,1500]{2,1,0:T(4,128)(2,1)} async-done(((bf16[10,4,1500]{2,1,0:T(4,128)(2,1)}), bf16[640,4,1500]{2,1,0:T(4,128)(2,1)}) %all-gather.3.cloned.1.call-update) | async-done | bytes 7680016 | tf_op jit(solution)/shard_map/all_gather | solution.py:14
  157.0 13.2 %reshape.60 = bf16[2560,1500]{1,0:T(8,128)(2,1)} reshape(bf16[640,4,1500]{2,1,0:T(4,128)(2,1)} %all-gather.3.cloned.1.call-done) | data formatting | bytes 15360000 | tf_op jit(solution)/shard_map/reshape | solution.py:17
  170.2 0.0 copy-done
  170.2 9.7 %convolution_convert_fusion = bf16[2560,640]{1,0:T(8,128)(2,1)} fusion(bf16[2560,1500]{1,0:T(8,128)(2,1)} %reshape.60, bf16[1500,1,640]{2,0,1:T(8,128)(2,1)S(1)} %copy-done), kind=kOutput, calls=%fused_computation | convolution fusion | flops 4916838400 | bytes 12876800 | tf_op jit(solution)/shard_map/dot_general | solution.py:16
  180.0 6.5 %reshape.62 = bf16[640,4,640]{2,1,0:T(4,128)(2,1)} reshape(bf16[2560,640]{1,0:T(8,128)(2,1)} %convolution_convert_fusion) | data formatting | bytes 6553600 | tf_op jit(solution)/shard_map/reshape | solution.py:21
  186.5 0.0 copy-start.1
  186.5 108.7 %all-gather.5.cloned.1.call-done = bf16[640,8,640]{2,1,0:T(8,128)(2,1)} async-done(((bf16[10,8,640]{2,1,0:T(8,128)(2,1)}), bf16[640,8,640]{2,1,0:T(8,128)(2,1)}) %all-gather.5.cloned.1.call-update) | async-done | bytes 6553616 | tf_op jit(solution)/shard_map/all_gather | solution.py:26
  295.2 8.2 %fusion.1 = f32[4,8,1]{0,1,2:T(8,128)S(1)} fusion(bf16[640,4,640]{2,1,0:T(4,128)(2,1)} %reshape.62, bf16[640,8,640]{2,1,0:T(8,128)(2,1)} %all-gather.5.cloned.1.call-done), kind=kOutput, calls=%fused_computation.5 | convolution fusion | flops 26214400 | bytes 9830528 | tf_op jit(solution)/shard_map/cxd,cid->xi/dot_general | solution.py:23
  303.3 9.0 %all-reduce = f32[4,1,8]{0,1,2:T(1,128)S(1)} all-reduce(f32[4,1,8]{0,1,2:T(1,128)S(1)} %bitcast.14), channel_id=2, replica_groups=mesh['vp'=64,'ch'=4] {'ch'}, use_global_device_ids=true, to_apply=%region_0.0.clone | all-reduce | flops 32 | bytes 256
  312.3 0.0 copy-done.1
  312.3 0.6 subtract_divide_fusion
  (1 shorter events, 0.0 us)
Async XLA Ops:
  6.5 163.7 %copy-start = (bf16[1500,1,640]{2,0,1:T(8,128)(2,1)S(1)}, bf16[1500,1,640]{2,0,1:T(8,128)(2,1)}, u32[]{:S(2)}) copy-start(bf16[1500,1,640]{2,0,1:T(8,128)(2,1)} %param.7) | copy-start | bytes 5760004
  6.5 150.5 %all-gather.3.cloned.1.call-start = ((), (), s32[]{:S(2)}) async-start(), calls=%async_computation | async-start | bytes 7987200 | tf_op jit(solution)/shard_map/all_gather | solution.py:14
  7.3 287.9 %all-gather.5.cloned.1.call-start = ((), (), s32[]{:S(2)}) async-start(), calls=%async_computation.1 | async-start | bytes 6656000 | tf_op jit(solution)/shard_map/all_gather | solution.py:26
  186.5 125.9 %copy-start.1 = (f32[2]{0:T(128)S(1)}, f32[2]{0:T(128)}, u32[]{:S(2)}) copy-start(f32[2]{0:T(128)} %param.11) | copy-start | bytes 28
Sparse Core Ops, SparseCore 0:
  11.0 145.9 all-gather.2
  160.5 134.6 all-gather.4
where the time goes:
time: 320 us
  waiting for transfers between devices  256 us (80%)
  local copies, waits for them, and re-layouts  21 us (7%)
  matrix products  17.9 us (6%)
  between operations  14.7 us (5%)
  blocking collectives  8.96 us (3%)
    all_gather x1, waiting for transfers between devices, body(): panel_rows = lax.all_gather(chol_a, 'vp', axis=0, tiled=True)  146 us
    all_gather x1, waiting for transfers between devices, body(): lax.all_gather(amplitudes, 'vp', axis=0, tiled=True)  109 us
    reshape x1, local copies, waits for them, and re-layouts, body(): panel_rows.reshape(rows_here * a_count, nch_dev)  13.2 us
    dot_general x1, matrix products, body(): jnp.dot(panel_rows.reshape(rows_here * a_count, nch_dev), cholesky_right,...  9.73 us
    unnamed x1, blocking collectives  8.96 us
    dot_general x1, matrix products, body(): jnp.einsum('cxd,cid->xi', v_rows, lax.all_gather(amplitudes, 'vp', axis=0...  8.17 us
    reshape x1, local copies, waits for them, and re-layouts, body(): v_rows.astype(jnp.bfloat16).reshape(rows_here, a_count * nb_dev, vir_count)  6.49 us
  transfers between devices with their start and end apart: 2, of which 2 were waited for; matrix products, arithmetic and copies ran while one was open for 10% of the time, Pallas kernels for 0%

commit v1 on v0

--- a/solution.py
+++ b/solution.py
@@ -1,7 +1,18 @@
+import functools
 import jax
 import jax.numpy as jnp
 from jax import lax
 from jax.sharding import PartitionSpec as P
+
+
+def _enter_unit(arr_in, dev_axis, out_dim):
+    carry_in = jnp.stack([arr_in] * jax.lax.psum(1, axis_name=dev_axis), axis=0)
+    return jnp.concatenate(
+        jax.lax.all_to_all(carry_in, axis_name=dev_axis, split_axis=0, concat_axis=0), axis=out_dim
+    )
+
+
+meet_seats_all_up = functools.partial(_enter_unit, dev_axis="vp", out_dim=0)
 
 
 def body(chol_a, chol_b, amplitudes, vir_a, vir_b, occ_pair):
@@ -21,10 +32,7 @@
     v_all = v_rows.astype(jnp.bfloat16).reshape(rows_here, a_count * nb_dev, vir_count)
     v_rows = v_all
     ladder = jnp.einsum(
-        "cxd,cid->xi",
-        v_rows,
-        lax.all_gather(amplitudes, "vp", axis=0, tiled=True),
-        preferred_element_type=jnp.float32,
+        "cxd,cid->xi", v_rows, meet_seats_all_up(amplitudes), preferred_element_type=jnp.float32
     )
     ladder = ladder.reshape(a_count, nb_dev, pair_count)
     ladder = lax.psum_scatter(ladder, "ch", scatter_dimension=2, tiled=True)

time: 320 us -> 264 us (0.82)
  waiting for transfers between devices: 256 us -> 182 us
  starting transfers between devices: 0.04 us -> 15.5 us
  local copies, waits for them, and re-layouts: 21 us -> 24.5 us
    all_gather x1 -> x0, waiting for transfers between devices: 109 us -> none  [body(): lax.all_gather(amplitudes, 'vp', axis=0, tiled=True)]
    all_gather x1, waiting for transfers between devices: 146 us -> 181 us  [body(): panel_rows = lax.all_gather(chol_a, 'vp', axis=0, tiled=True)]
    all_to_all x0 -> x1, starting transfers between devices: none -> 15.5 us  [_enter_unit(): jax.lax.all_to_all(carry_in, axis_name=dev_axis, split_axis=0, concat_axi...]
    another operation x0 -> x1, local copies, waits for them, and re-layouts: none -> 4.14 us  [_enter_unit(): carry_in = jnp.stack([arr_in] * jax.lax.psum(1, axis_name=dev_axis), axis=0)]
  transfers between devices with their start and end apart: 2 -> 2, of which waited for: 2 -> 1; matrix products, arithmetic and copies ran while one was open for 10% -> 13% of each run, Pallas kernels for 0% -> 0%
where the time goes in v1:
time: 264 us; the launch traced here: 262 us
  waiting for transfers between devices  182 us (69%)
  local copies, waits for them, and re-layouts  24.5 us (9%)
  matrix products  18 us (7%)
  starting transfers between devices  15.5 us (6%)
  between operations  14.7 us (6%)
  blocking collectives  6.74 us (3%)
    all_gather x1, waiting for transfers between devices, body(): panel_rows = lax.all_gather(chol_a, 'vp', axis=0, tiled=True)  181 us
    all_to_all x1, starting transfers between devices, _enter_unit(): jax.lax.all_to_all(carry_in, axis_name=dev_axis, split_axis=0, concat_axi...  15.5 us
    reshape x1, local copies, waits for them, and re-layouts, body(): panel_rows.reshape(rows_here * a_count, nch_dev)  13.2 us
    dot_general x1, matrix products, body(): jnp.dot(panel_rows.reshape(rows_here * a_count, nch_dev), cholesky_right,...  9.78 us
    dot_general x1, matrix products, body(): jnp.einsum('cxd,cid->xi', v_rows, meet_seats_all_up(amplitudes), preferre...  8.17 us
    unnamed x1, blocking collectives  6.74 us
    reshape x1, local copies, waits for them, and re-layouts, body(): v_rows.astype(jnp.bfloat16).reshape(rows_here, a_count * nb_dev, vir_count)  6.49 us
  transfers between devices with their start and end apart: 2, of which 1 were waited for; matrix products, arithmetic and copies ran while one was open for 13% of the time, Pallas kernels for 0%

profile of v1, /device:TPU:1, one launch (start us, length us, event | category | flops | bytes accessed | tf_op | source)
XLA Modules:
  0.0 262.0 jit_solution(14730057927409799869)
XLA Ops:
  6.5 0.0 copy-start
  6.5 0.0 all-gather.2.cloned.1.call-start
  6.5 0.7 all-gather.2.cloned.1.call-update
  7.3 4.1 %stack.2 = bf16[64,10,8,640]{3,2,1,0:T(8,128)(2,1)} broadcast(bf16[10,8,640]{2,1,0:T(8,128)(2,1)} %param.8), dimensions={1,2,3} | broadcast | bytes 6656000 | tf_op jit(solution)/shard_map/stack | solution.py:9
  11.4 0.0 copy-start.3
  11.4 0.0 copy-start.2
  11.4 15.5 %all-to-all-start = ((bf16[64,10,8,640]{3,2,1,0:T(8,128)(2,1)}), bf16[64,10,8,640]{3,2,1,0:T(8,128)(2,1)}, u32[]{:S(2)}, u32[]{:S(2)}) async-start(bf16[64,10,8,640]{3,2,1,0:T(8,128)(2,1)} %stack.2), calls=%async_computation | async-start | bytes 13107200 | tf_op jit(solution)/shard_map/all_to_all | solution.py:11
  27.5 0.0 copy-done.3
  27.6 0.6 dynamic-slice
  28.8 0.0 copy-done.2
  28.8 181.2 %all-gather.2.cloned.1.call-done = bf16[640,4,1500]{2,1,0:T(4,128)(2,1)} async-done(((bf16[10,4,1500]{2,1,0:T(4,128)(2,1)}), bf16[640,4,1500]{2,1,0:T(4,128)(2,1)}) %all-gather.2.cloned.1.call-update) | async-done | bytes 7680016 | tf_op jit(solution)/shard_map/all_gather | solution.py:25
  210.1 13.2 %reshape.65 = bf16[2560,1500]{1,0:T(8,128)(2,1)} reshape(bf16[640,4,1500]{2,1,0:T(4,128)(2,1)} %all-gather.2.cloned.1.call-done) | data formatting | bytes 15360000 | tf_op jit(solution)/shard_map/reshape | solution.py:28
  223.3 0.0 copy-done
  223.3 9.8 %convolution_convert_fusion = bf16[2560,640]{1,0:T(8,128)(2,1)} fusion(bf16[2560,1500]{1,0:T(8,128)(2,1)} %reshape.65, bf16[1500,1,640]{2,0,1:T(8,128)(2,1)S(1)} %copy-done), kind=kOutput, calls=%fused_computation | convolution fusion | flops 4916838400 | bytes 12876800 | tf_op jit(solution)/shard_map/dot_general | solution.py:27
  233.1 6.5 %reshape.67 = bf16[640,4,640]{2,1,0:T(4,128)(2,1)} reshape(bf16[2560,640]{1,0:T(8,128)(2,1)} %convolution_convert_fusion) | data formatting | bytes 6553600 | tf_op jit(solution)/shard_map/reshape | solution.py:32
  239.6 0.0 copy-start.1
  239.6 0.0 all-to-all-done
  239.6 8.2 %fusion.1 = f32[4,8,1]{0,1,2:T(8,128)S(1)} fusion(bf16[640,4,640]{2,1,0:T(4,128)(2,1)} %reshape.67, bf16[640,8,640]{2,1,0:T(8,128)(2,1)} %bitcast.1), kind=kOutput, calls=%fused_computation.5 | convolution fusion | flops 26214400 | bytes 9830528 | tf_op jit(solution)/shard_map/cxd,cid->xi/dot_general | solution.py:34
  247.7 6.7 %all-reduce = f32[4,1,8]{0,1,2:T(1,128)S(1)} all-reduce(f32[4,1,8]{0,1,2:T(1,128)S(1)} %bitcast.15), channel_id=2, replica_groups=mesh['vp'=64,'ch'=4] {'ch'}, use_global_device_ids=true, to_apply=%region_0.0.clone | all-reduce | flops 32 | bytes 256
  254.5 0.0 copy-done.1
  254.5 0.6 subtract_divide_fusion
  (2 shorter events, 0.0 us)
Async XLA Ops:
  6.5 216.7 %copy-start = (bf16[1500,1,640]{2,0,1:T(8,128)(2,1)S(1)}, bf16[1500,1,640]{2,0,1:T(8,128)(2,1)}, u32[]{:S(2)}) copy-start(bf16[1500,1,640]{2,0,1:T(8,128)(2,1)} %param.7) | copy-start | bytes 5760004
  6.5 203.5 %all-gather.2.cloned.1.call-start = ((), (), s32[]{:S(2)}) async-start(), calls=%async_computation.1 | async-start | bytes 7987200 | tf_op jit(solution)/shard_map/all_gather | solution.py:25
  11.4 16.1 %copy-start.3 = (u32[256]{0:T(256)S(1)}, u32[256]{0:T(256)}, u32[]{:S(2)}) copy-start(u32[256]{0:T(256)} %constant.7) | copy-start | bytes 3076
  11.4 17.4 %copy-start.2 = (f32[4]{0:T(128)S(1)}, f32[4]{0:T(128)}, u32[]{:S(2)}) copy-start(f32[4]{0:T(128)} %param.9) | copy-start | bytes 52
  11.4 228.1 %all-to-all-start = ((bf16[64,10,8,640]{3,2,1,0:T(8,128)(2,1)}), bf16[64,10,8,640]{3,2,1,0:T(8,128)(2,1)}, u32[]{:S(2)}, u32[]{:S(2)}) async-start(bf16[64,10,8,640]{3,2,1,0:T(8,128)(2,1)} %stack.2), calls=%async_computation | async-start | bytes 13107200 | tf_op jit(solution)/shard_map/all_to_all | solution.py:11
  239.6 14.9 %copy-start.1 = (f32[2]{0:T(128)S(1)}, f32[2]{0:T(128)}, u32[]{:S(2)}) copy-start(f32[2]{0:T(128)} %param.11) | copy-start | bytes 28
Sparse Core Ops, SparseCore 0:
  11.0 198.9 all-gather.1
